TPU v7x, 32 devices: a whole 2x2x4 slice. The times are simulated.
32 devices in a mesh: wide: 16 (over z, y, x), narrow: 2 (over core).
Axes of the slice: x: 2, y: 2, z: 4, core: 2. Of those that a mesh axis runs over, the one named last changes fastest.
Arguments:
- tokens: bfloat16 [1024, 2048], P('wide'), may hold values from -6 to 6
- routes: int32 [1024, 6], P('wide'), may hold values from 0 to 15, all different within a row; in each aligned block of 64 rows (0 to 63, 64 to 127, ...) at most 44 rows name the same one
- route_weight: float32 [1024, 6], P('wide'), may hold values from 0.1 to 0.8
- w_gate: bfloat16 [16, 1408, 2048], P('wide', None, 'narrow'), may hold values from -0.1875 to 0.1875
- w_up: bfloat16 [16, 1408, 2048], P('wide', None, 'narrow'), may hold values from -0.1875 to 0.1875
- w_down: bfloat16 [16, 1408, 2048], P('wide', None, 'narrow'), may hold values from -0.15625 to 0.15625
Outputs:
- combined: bfloat16 [1024, 2048], P('wide', 'narrow')
Inputs may be any that keep to these rules, and one draw needn't show every extreme that they name: `routes`: each row names 6 different experts. Within each aligned block of 64 rows no expert is named by more than 44 rows, and in some block an expert is named by exactly 44 rows.
All inputs are finite; a program needn't handle non-finite values.
Results may differ from a plain program's by a relative error of at most 0.029.
Values may be sent and summed in bfloat16 or wider, within the bound.
A program may use at most 64 MiB of HBM per device.

v0:
```python
import jax
import jax.numpy as jnp
from jax import lax
from jax.sharding import PartitionSpec as P


def slot_numbers(routes, experts):
    flat_routes = routes.reshape(-1)
    onehot = (flat_routes[:, None] == jnp.arange(experts, dtype=jnp.int32)[None, :]).astype(
        jnp.int32
    )
    before = jnp.cumsum(onehot, 0) - onehot
    return jnp.sum(before * onehot, 1).reshape(routes.shape)


def on_device(tokens, routes, route_weight, w_gate, w_up, w_down):
    tok_count = tokens.shape[0]
    model_width = tokens.shape[1]
    wide_count = lax.axis_size("wide")
    narrow_count = lax.axis_size("narrow")
    local_experts = w_gate.shape[0]
    experts = local_experts * wide_count
    capacity = max(2, (11 * tok_count + experts - 1) // experts)
    column_width = model_width // narrow_count
    slot_index = slot_numbers(routes, experts)
    target = routes * capacity + slot_index
    lane_ids = jnp.arange(experts * capacity, dtype=jnp.int32)
    picker = jnp.sum((lane_ids[:, None, None] == target[None, :, :]).astype(jnp.int32), 2).astype(
        jnp.bfloat16
    )
    columns = lax.dynamic_slice_in_dim(
        tokens, lax.axis_index("narrow") * column_width, column_width, 1
    )
    outgoing = jnp.dot(picker, columns, preferred_element_type=jnp.float32).astype(jnp.bfloat16)
    outgoing = outgoing.reshape(experts, capacity, column_width)
    received = lax.all_to_all(outgoing, "wide", split_axis=0, concat_axis=1, tiled=True)
    expert_rows = received[0]
    slot_total = expert_rows.shape[0]
    gate_matrix = w_gate[0]
    up_matrix = w_up[0]
    down_matrix = w_down[0]
    gate_term = jnp.einsum(
        "sc,fc->fs", expert_rows, gate_matrix, preferred_element_type=jnp.float32
    )
    up_term = jnp.einsum("sc,fc->fs", expert_rows, up_matrix, preferred_element_type=jnp.float32)
    sums = lax.psum_scatter(
        jnp.concatenate([gate_term, up_term], 1).astype(jnp.bfloat16),
        "narrow",
        scatter_dimension=0,
        tiled=True,
    ).astype(jnp.float32)
    hidden = (jax.nn.silu(sums[:, :slot_total]) * sums[:, slot_total:]).astype(jnp.bfloat16)
    produced = jnp.einsum(
        "fs,fc->sc",
        lax.all_gather(hidden, "narrow", axis=0, tiled=True),
        down_matrix,
        preferred_element_type=jnp.float32,
    )
    expert_out = produced.astype(jnp.bfloat16).reshape(local_experts, slot_total, column_width)
    returned = lax.all_to_all(expert_out, "wide", split_axis=1, concat_axis=0, tiled=True)
    flat_rows = returned.reshape(experts * capacity, column_width)
    picked = jnp.take(flat_rows, target, axis=0).astype(jnp.float32)
    combined = jnp.sum(picked * route_weight[:, :, None], 1)
    return combined.astype(jnp.bfloat16)


def solution(mesh):
    return jax.shard_map(
        on_device,
        mesh=mesh,
        in_specs=(
            P("wide", None),
            P("wide", None),
            P("wide", None),
            P("wide", None, "narrow"),
            P("wide", None, "narrow"),
            P("wide", None, "narrow"),
        ),
        out_specs=P("wide", "narrow"),
        check_vma=False,
    )
```

profile of v0, /device:TPU:0, one launch (start us, length us, event | category | flops | bytes accessed | tf_op | source)
XLA Modules:
  0.0 207.4 jit_solution(14892390840280336226)
XLA Ops:
  6.5 0.9 copy.41
  7.8 0.9 reduce-window.6
  8.6 0.2 slice_reduce_fusion
  9.0 0.1 reshape.45
  9.2 0.7 compare_and_fusion
  9.9 0.2 convert_reduce_fusion
  10.1 2.6 %convolution_convert_fusion.2 = bf16[704,1024]{1,0:T(8,128)(2,1)} fusion(bf16[64,2048]{1,0:T(8,128)(2,1)} %param.6, s32[]{:T(128)S(6)} %select_n.13, s32[704,64]{0,1:T(8,128)S(1)} %convert_reduce_fusion), kind=kOutput, calls=%fused_computation.14 | convolution fusion | flops 93040640 | bytes 1753092 | tf_op jit(solution)/shard_map/dot_general | solution.py:34
  12.7 3.3 %reshape.46 = bf16[16,44,1024]{2,1,0:T(8,128)(2,1)} reshape(bf16[704,1024]{1,0:T(8,128)(2,1)} %convolution_convert_fusion.2) | data formatting | bytes 2883584 | tf_op jit(solution)/shard_map/reshape | solution.py:35
  16.0 46.0 %all_to_all.8 = bf16[16,44,1024]{2,1,0:T(8,128)(2,1)} all-to-all(bf16[16,44,1024]{2,1,0:T(8,128)(2,1)} %reshape.46), channel_id=1, replica_groups=mesh['wide'=16,'narrow'=2] {'wide'}, dimensions={0} | all-to-all | bytes 2883584 | tf_op jit(solution)/shard_map/all_to_all | solution.py:36
  62.0 3.3 %squeeze.12 = bf16[704,1024]{1,0:T(8,128)(2,1)} reshape(bf16[16,44,1024]{2,1,0:T(8,128)(2,1)} %all_to_all.8) | data formatting | bytes 2883584 | tf_op jit(solution)/shard_map/squeeze | solution.py:37
  65.3 3.9 %fusion = bf16[1408,704]{0,1:T(8,128)(2,1)S(1)} fusion(bf16[704,1024]{1,0:T(8,128)(2,1)} %squeeze.12, bf16[1,1408,1024]{2,1,0:T(8,128)(2,1)S(1)} %copy-done), kind=kOutput, calls=%fused_computation.4 | convolution fusion | flops 2031034368 | bytes 6307840 | tf_op jit(solution)/shard_map/sc,fc->fs/dot_general | solution.py:42
  69.3 2.4 %fusion.1 = bf16[1408,704]{0,1:T(8,128)(2,1)S(1)} fusion(bf16[704,1024]{1,0:T(8,128)(2,1)S(1)} %copy-done.1, bf16[1,1408,1024]{2,1,0:T(8,128)(2,1)S(1)} %copy-done.3), kind=kOutput, calls=%fused_computation.5 | convolution fusion | flops 2031034368 | bytes 6307840 | tf_op jit(solution)/shard_map/sc,fc->fs/dot_general | solution.py:45
  71.7 2.2 %pad_maximum_fusion = bf16[1408,1408]{0,1:T(8,128)(2,1)} fusion(bf16[1408,704]{0,1:T(8,128)(2,1)S(1)} %fusion.1, bf16[1408,704]{0,1:T(8,128)(2,1)S(1)} %fusion), kind=kLoop, calls=%fused_computation.1 | loop fusion | flops 7929856 | bytes 7929856 | tf_op jit(solution)/shard_map/concatenate | solution.py:47
  73.9 6.2 %copy.50 = bf16[1408,1408]{1,0:T(8,128)(2,1)} copy(bf16[1408,1408]{0,1:T(8,128)(2,1)} %pad_maximum_fusion) | data formatting | bytes 7929856
  80.2 10.3 %reduce-scatter.4.cloned.1.call-done = bf16[704,1408]{1,0:T(8,128)(2,1)} async-done(((bf16[1408,1408]{1,0:T(8,128)(2,1)}), bf16[704,1408]{1,0:T(8,128)(2,1)}) %reduce-scatter.4.cloned.1.call-update) | async-done | bytes 1982480
  90.5 4.0 %copy.51 = bf16[704,1408]{0,1:T(8,128)(2,1)} copy(bf16[704,1408]{1,0:T(8,128)(2,1)} %reduce-scatter.4.cloned.1.call-done) | data formatting | bytes 3964928
  94.5 1.9 convert_element_type.37
  96.5 1.6 fusion.6
  98.1 2.3 %copy.46 = bf16[704,704]{1,0:T(8,128)(2,1)} copy(bf16[704,704]{0,1:T(8,128)(2,1)} %fusion.6) | data formatting | bytes 1982464 | tf_op jit(solution)/shard_map/convert_element_type | solution.py:52
  100.5 12.1 %all-gather.2.cloned.1.call-done = bf16[1408,704]{1,0:T(8,128)(2,1)} async-done(((bf16[704,704]{1,0:T(8,128)(2,1)}), bf16[1408,704]{1,0:T(8,128)(2,1)}) %all-gather.2.cloned.1.call-update) | async-done | bytes 1982480 | tf_op jit(solution)/shard_map/all_gather | solution.py:55
  112.6 4.9 %fusion.10 = bf16[1,704,1024]{2,1,0:T(8,128)(2,1)S(1)} fusion(bf16[1408,704]{1,0:T(8,128)(2,1)} %all-gather.2.cloned.1.call-done, bf16[1,1408,1024]{2,1,0:T(8,128)(2,1)} %param.11), kind=kOutput, calls=%fused_computation.15 | convolution fusion | flops 2030764032 | bytes 6307840 | tf_op jit(solution)/shard_map/fs,fc->sc/dot_general | solution.py:53
  117.5 3.8 %copy.58 = bf16[1,704,1024]{2,0,1:T(2,128)(2,1)} copy(bf16[1,704,1024]{2,1,0:T(8,128)(2,1)S(1)} %fusion.10) | data formatting | bytes 2883584 | tf_op jit(solution)/shard_map/reshape | solution.py:59
  121.3 0.5 broadcast.31
  121.8 11.8 %reduce.2 = bf16[704,1024]{1,0:T(8,128)(2,1)} reduce(bf16[704,1,1024]{2,1,0:T(2,128)(2,1)} %bitcast.51, bf16[]{:T(256)} %broadcast.31), dimensions={1}, to_apply=%bitcast.48.reduce_sub_computation | reduce | bytes 2883586
  133.6 4.6 %reshape.62 = bf16[16,2,22528]{2,1,0:T(2,128)(2,1)} reshape(bf16[704,1024]{1,0:T(8,128)(2,1)} %reduce.2) | data formatting | bytes 2883584
  138.2 7.0 %all-to-all-start.1 = ((bf16[16,2,22528]{2,1,0:T(2,128)(2,1)}), bf16[16,2,22528]{2,1,0:T(2,128)(2,1)}, u32[]{:S(2)}, u32[]{:S(2)}) async-start(bf16[16,2,22528]{2,1,0:T(2,128)(2,1)} %reshape.62), calls=%async_computation.1 | async-start | bytes 2883584 | tf_op jit(solution)/shard_map/all_to_all | solution.py:60
  145.6 31.6 %all-to-all-done.1 = bf16[16,2,22528]{2,1,0:T(2,128)(2,1)} async-done(((bf16[16,2,22528]{2,1,0:T(2,128)(2,1)}), bf16[16,2,22528]{2,1,0:T(2,128)(2,1)}, u32[]{:S(2)}, u32[]{:S(2)}) %all-to-all-start.1) | async-done | bytes 1441824 | tf_op jit(solution)/shard_map/all_to_all | solution.py:60
  177.3 9.9 %reshape.63 = bf16[704,1,1024]{2,1,0:T(2,128)(2,1)} reshape(bf16[16,2,22528]{2,1,0:T(2,128)(2,1)} %all-to-all-done.1) | data formatting | bytes 2883584
  187.2 3.5 %copy.57 = bf16[1,704,1024]{2,1,0:T(8,128)(2,1)} copy(bf16[1,704,1024]{2,0,1:T(2,128)(2,1)} %bitcast.52) | data formatting | bytes 2883584
  190.7 4.9 %gather_fusion = bf16[384,1024]{1,0:T(8,128)(2,1)} fusion(bf16[704,1024]{1,0:T(8,128)(2,1)} %bitcast.50, s32[1024]{0:T(1024)S(1)} %pad_clamp_fusion), kind=kCustom, calls=%fused_computation | custom fusion | bytes 1574400 | tf_op jit(solution)/shard_map/jit(_take)/gather | solution.py:62
  195.6 2.2 %reshape.50 = bf16[64,6,1024]{2,1,0:T(8,128)(2,1)} reshape(bf16[384,1024]{1,0:T(8,128)(2,1)} %gather_fusion) | data formatting | bytes 1572864 | tf_op jit(solution)/shard_map/jit(_take)/gather | solution.py:62
  197.8 2.8 %multiply_reduce_fusion = bf16[64,1024]{1,0:T(8,128)(2,1)} fusion(f32[64,6]{1,0:T(8,128)S(1)} %copy.49, bf16[64,6,1024]{2,1,0:T(8,128)(2,1)} %reshape.50, pred[64,6]{1,0:T(8,128)(4,1)S(1)} %copy.45), kind=kLoop, calls=%fused_computation.12 | loop fusion | flops 1507328 | bytes 919424 | tf_op jit(solution)/shard_map/reduce_sum | solution.py:63
  (24 shorter events, 1.0 us)
Async XLA Ops:
  6.5 58.7 %copy-start = (bf16[1,1408,1024]{2,1,0:T(8,128)(2,1)S(1)}, bf16[1,1408,1024]{2,1,0:T(8,128)(2,1)}, u32[]{:S(2)}) copy-start(bf16[1,1408,1024]{2,1,0:T(8,128)(2,1)} %param.9) | copy-start | bytes 8650756
  6.5 83.9 %reduce-scatter.4.cloned.1.call-start = ((), (), s32[]{:S(2)}) async-start(), calls=%async_computation.4 | async-start | bytes 5947392
  65.3 4.0 %copy-start.1 = (bf16[704,1024]{1,0:T(8,128)(2,1)S(1)}, bf16[704,1024]{1,0:T(8,128)(2,1)}, u32[]{:S(2)}) copy-start(bf16[704,1024]{1,0:T(8,128)(2,1)} %squeeze.12) | copy-start | bytes 4325380
  65.3 4.0 %copy-start.3 = (bf16[1,1408,1024]{2,1,0:T(8,128)(2,1)S(1)}, bf16[1,1408,1024]{2,1,0:T(8,128)(2,1)}, u32[]{:S(2)}) copy-start(bf16[1,1408,1024]{2,1,0:T(8,128)(2,1)} %param.10) | copy-start | bytes 8650756
  80.2 32.4 %all-gather.2.cloned.1.call-start = ((), (), s32[]{:S(2)}) async-start(), calls=%async_computation.3 | async-start | bytes 3244032 | tf_op jit(solution)/shard_map/all_gather | solution.py:55
  138.2 7.3 %copy-start.2 = (f32[64,6]{0,1:T(8,128)S(1)}, f32[64,6]{0,1:T(8,128)}, u32[]{:S(2)}) copy-start(f32[64,6]{0,1:T(8,128)} %param.8) | copy-start | bytes 4612
  138.2 39.1 %all-to-all-start.1 = ((bf16[16,2,22528]{2,1,0:T(2,128)(2,1)}), bf16[16,2,22528]{2,1,0:T(2,128)(2,1)}, u32[]{:S(2)}, u32[]{:S(2)}) async-start(bf16[16,2,22528]{2,1,0:T(2,128)(2,1)} %reshape.62), calls=%async_computation.1 | async-start | bytes 2883584 | tf_op jit(solution)/shard_map/all_to_all | solution.py:60
Sparse Core Ops, SparseCore 0:
  80.3 10.1 reduce-scatter.3
  100.6 11.9 all-gather.1
where the time goes:
time: 210 us; the launch traced here: 207 us
  waiting for transfers between devices  54.1 us (26%)
  local copies, waits for them, and re-layouts  50.7 us (24%)
  blocking collectives  46 us (22%)
  other arithmetic  22.2 us (11%)
  matrix products  13.8 us (7%)
  between operations  13.5 us (6%)
  starting transfers between devices  7 us (3%)
    all_to_all x1, blocking collectives, on_device(): lax.all_to_all(outgoing, 'wide', split_axis=0, concat_axis=1, tiled=True)  46 us
    all_to_all x1, waiting for transfers between devices, on_device(): lax.all_to_all(expert_out, 'wide', split_axis=1, concat_axis=0, tiled=True)  31.6 us
    unnamed x16, local copies, waits for them, and re-layouts  29.8 us
    all_gather x1, waiting for transfers between devices, on_device(): lax.all_gather(hidden, 'narrow', axis=0, tiled=True)  12.1 us
    unnamed x1, other arithmetic  11.8 us
    unnamed x3, waiting for transfers between devices  10.3 us
    gather x2, local copies, waits for them, and re-layouts, on_device(): picked = jnp.take(flat_rows, target, axis=0).astype(jnp.float32)  7.12 us
    all_to_all x1, starting transfers between devices, on_device(): lax.all_to_all(expert_out, 'wide', split_axis=1, concat_axis=0, tiled=True)  6.96 us
  transfers between devices with their start and end apart: 3, of which 3 were waited for; matrix products, arithmetic and copies ran while one was open for 0% of the time, Pallas kernels for 0%

commit v1 on v0

--- a/solution.py
+++ b/solution.py
@@ -1,6 +1,10 @@
+import functools
+
 import jax
 import jax.numpy as jnp
 from jax import lax
+from jax.experimental import pallas as pl
+from jax.experimental.pallas import tpu as pltpu
 from jax.sharding import PartitionSpec as P
 
 
@@ -13,7 +17,7 @@
     return jnp.sum(before * onehot, 1).reshape(routes.shape)
 
 
-def on_device(tokens, routes, route_weight, w_gate, w_up, w_down):
+def slots_plan(tokens, routes, route_weight, w_gate, w_up, w_down):
     tok_count = tokens.shape[0]
     model_width = tokens.shape[1]
     wide_count = lax.axis_size("wide")
@@ -64,9 +68,314 @@
     return combined.astype(jnp.bfloat16)
 
 
+WAVES = 2
+NT = (((1,), (1,)), ((), ()))
+NN = (((1,), (0,)), ((), ()))
+
+
+def place(column, z):
+    return (z // 2) * 8 + column * 2 + z % 2
+
+
+def kernel(
+    tokens, routes, weights, gate_hbm, up_hbm, down_hbm, out,
+    tok, gate_up, down, coef, scale, gsend, grecv, hid, part, back, zsend, zrecv,
+    load_sem, own_sem, ag_send, ag_recv, cf_send, cf_recv,
+    g_send, g_recv, h_send, h_recv, rs_send, rs_recv, z_send, z_recv,
+):
+    w = lax.axis_index("wide")
+    n = lax.axis_index("narrow")
+    z = w // 4
+    x_peer = w + 1 - 2 * (w % 2)
+    y_peer = w + 2 - 4 * ((w // 2) % 2)
+    tiles = gate_up.shape[0]
+    rows = tok.shape[2]
+    half_rows = 8 * rows
+    cols = tok.shape[3]
+
+    def copy(src, dst, send, recv, wide, narrow=n):
+        return pltpu.make_async_remote_copy(
+            src_ref=src, dst_ref=dst, send_sem=send, recv_sem=recv,
+            device_id=(wide, narrow), device_id_type=pl.DeviceIdType.MESH,
+        )
+
+    def arrived(dst, recv, wide=x_peer):
+        copy(dst, dst, recv, recv, wide).wait_recv()
+
+    sent = []
+
+    def send(src, dst, send_sem, recv_sem, wide, narrow=n):
+        c = copy(src, dst, send_sem, recv_sem, wide, narrow)
+        c.start()
+        sent.append(c)
+
+    def z_peer(k):
+        return (w + 4 * k) % 16
+
+    barrier = pltpu.get_barrier_semaphore()
+    for wide, narrow in [(z_peer(k), n) for k in (1, 2, 3)] + [(x_peer, n), (y_peer, n), (w, 1 - n)]:
+        pl.semaphore_signal(barrier, inc=1, device_id=(wide, narrow), device_id_type=pl.DeviceIdType.MESH)
+    loads = [
+        pltpu.make_async_copy(gate_hbm, gate_up.at[:, 0], load_sem.at[0]),
+        pltpu.make_async_copy(up_hbm, gate_up.at[:, 1], load_sem.at[1]),
+        pltpu.make_async_copy(down_hbm, down, load_sem.at[2]),
+    ]
+    own_block = [tokens.at[pl.ds(v * rows, rows), pl.ds(pl.multiple_of(n * cols, cols), cols)] for v in range(WAVES)]
+    own_copy = [
+        pltpu.make_async_copy(own_block[v], tok.at[v, place(0, z)], own_sem.at[v]) for v in range(WAVES)
+    ]
+    pl.semaphore_wait(barrier, 6)
+
+    def send_z(v):
+        for k in (1, 3, 2):
+            send(own_block[v], tok.at[v, place(0, z)], ag_send.at[v, 0, k], ag_recv.at[v, 0, z], z_peer(k))
+
+    def send_xy(v, src, from_z):
+        send(src, tok.at[v, place(1, from_z)], ag_send.at[v, 1, from_z], ag_recv.at[v, 1, from_z], x_peer)
+        send(src, tok.at[v, place(2, from_z)], ag_send.at[v, 2, from_z], ag_recv.at[v, 2, from_z], y_peer)
+
+    def pass_column(v):
+        for k in (1, 3, 2):
+            from_z = (z + k) % 4
+            block = tok.at[v, place(0, from_z)]
+            arrived(block, ag_recv.at[v, 0, from_z])
+            send_xy(v, block, from_z)
+
+    def pass_diagonal(v):
+        for low in (0, 1):
+            for h in (0, 1):
+                from_z = 2 * h + low
+                block = tok.at[v, place(1 + h, from_z)]
+                arrived(block, ag_recv.at[v, 1 + h, from_z])
+                send(
+                    block, tok.at[v, place(3, from_z)], ag_send.at[v, 3, from_z], ag_recv.at[v, 3, from_z],
+                    y_peer if h == 0 else x_peer,
+                )
+
+    def gather_rest(v):
+        for low in (0, 1):
+            for h in (0, 1):
+                from_z = 2 * h + low
+                arrived(tok.at[v, place(2 - h, from_z)], ag_recv.at[v, 2 - h, from_z])
+                arrived(tok.at[v, place(3, from_z)], ag_recv.at[v, 3, from_z])
+        own_copy[v].wait()
+
+    send_z(0)
+    send_xy(0, own_block[0], z)
+    send_z(1)
+    for c in own_copy + loads:
+        c.start()
+
+    lane = lax.broadcasted_iota(jnp.int32, (8, 128), 1)
+    packed = jnp.zeros((8, 128), jnp.float32)
+    for g in range(tokens.shape[0] // 8):
+        for k in range(routes.shape[1]):
+            chosen = routes[pl.ds(8 * g, 8), k : k + 1] + 16 * g
+            packed += jnp.where(lane == chosen, weights[pl.ds(8 * g, 8), k : k + 1], 0.0)
+    coef[0, z] = packed
+    for k in (1, 2, 3):
+        send(coef.at[0, z], coef.at[0, z], cf_send.at[k], cf_recv.at[z], z_peer(k))
+
+    pass_column(0)
+    send_xy(1, own_block[1], z)
+    pass_diagonal(0)
+    pass_column(1)
+    for k in (1, 2, 3):
+        from_z = (z + k) % 4
+        arrived(coef.at[0, from_z], cf_recv.at[from_z])
+    send(coef.at[0], coef.at[1], cf_send.at[4], cf_recv.at[4], x_peer)
+    send(coef.at[0], coef.at[2], cf_send.at[5], cf_recv.at[5], y_peer)
+    for c in loads[:2]:
+        c.wait()
+    gather_rest(0)
+
+    def tile(i):
+        return gate_up[i].reshape(2 * gate_up.shape[2], cols)
+
+    def half(v, h):
+        return tok[v, pl.ds(8 * h, 8)].reshape(half_rows, cols)
+
+    def partner_sums(v):
+        @pl.loop(0, tiles)
+        def _(i):
+            sums = lax.dot_general(half(v, 1 - n), tile(i), NT, preferred_element_type=jnp.float32)
+            gsend[v, i] = sums.astype(jnp.bfloat16)
+            copy(gsend.at[v, i], grecv.at[v, i], g_send.at[v, i], g_recv.at[v, i], w, 1 - n).start()
+
+    def own_hidden(v):
+        @pl.loop(0, tiles)
+        def _(i):
+            sums = lax.dot_general(half(v, n), tile(i), NT, preferred_element_type=jnp.float32)
+            arrived(grecv.at[v, i], g_recv.at[v, i])
+            sums += grecv[v, i].astype(jnp.float32)
+            gate, up = sums[:, :128], sums[:, 128:]
+            lanes = pl.ds(pl.multiple_of(i * 128, 128), 128)
+            hid[v, n, :, lanes] = (gate / (1.0 + jnp.exp(-gate)) * up).astype(jnp.bfloat16)
+            there = hid.at[v, n, :, lanes]
+            copy(there, there, h_send.at[v, i], h_recv.at[v, i], w, 1 - n).start()
+
+    def outputs(v, h):
+        column = scale[v, pl.ds(8 * h, 8)].reshape(half_rows, 128)[:, 0:1]
+
+        @pl.loop(0, cols // 256)
+        def _(i):
+            lanes = pl.ds(pl.multiple_of(i * 256, 256), 256)
+            acc = lax.dot_general(hid[v, h], down[:, lanes], NN, preferred_element_type=jnp.float32)
+            part[v, pl.ds(8 * h, 8), :, lanes] = (acc * column).astype(jnp.bfloat16).reshape(8, rows, 256)
+
+    def other_hidden(v):
+        @pl.loop(0, tiles)
+        def _(i):
+            lanes = pl.ds(pl.multiple_of(i * 128, 128), 128)
+            arrived(hid.at[v, 1 - n, :, lanes], h_recv.at[v, i])
+
+    def send_half(v, h):
+        peer = x_peer + h * (y_peer - x_peer)
+        for low in (0, 1):
+            at = 2 * h + low
+            send(part.at[v, place(3, at)], back.at[v, 0, at], rs_send.at[v, 0, at], rs_recv.at[v, 0, at], peer)
+        for low in (0, 1):
+            at = 2 * h + low
+            send(
+                part.at[v, place(1 + h, at)], back.at[v, 1 + h, at],
+                rs_send.at[v, 1 + h, at], rs_recv.at[v, 1 + h, at], peer,
+            )
+
+    def relay_sums(v):
+        for low in (0, 1):
+            for h in (0, 1):
+                at = 2 * h + low
+                arrived(back.at[v, 0, at], rs_recv.at[v, 0, at])
+                mine = part[v, place(2 - h, at)].astype(jnp.float32)
+                part[v, place(2 - h, at)] = (mine + back[v, 0, at].astype(jnp.float32)).astype(jnp.bfloat16)
+                send(
+                    part.at[v, place(2 - h, at)], back.at[v, 2 - h, at],
+                    rs_send.at[v, 2 - h, at], rs_recv.at[v, 2 - h, at], y_peer if h == 0 else x_peer,
+                )
+
+    def column_sums(v):
+        for k in (2, 1, 3, 0):
+            at = (z + k) % 4
+            arrived(back.at[v, 1, at], rs_recv.at[v, 1, at])
+            arrived(back.at[v, 2, at], rs_recv.at[v, 2, at])
+            total = part[v, place(0, at)].astype(jnp.float32)
+            total += back[v, 1, at].astype(jnp.float32) + back[v, 2, at].astype(jnp.float32)
+            if k == 0:
+                zrecv[v, z] = total.astype(jnp.bfloat16)
+            else:
+                zsend[v, k] = total.astype(jnp.bfloat16)
+                send(zsend.at[v, k], zrecv.at[v, z], z_send.at[v, k], z_recv.at[v, z], z_peer(k))
+
+    def finish(v):
+        for k in (1, 3, 2):
+            at = (z + k) % 4
+            arrived(zrecv.at[v, at], z_recv.at[v, at])
+        total = zrecv[v, 0].astype(jnp.float32) + zrecv[v, 1].astype(jnp.float32)
+        total += zrecv[v, 2].astype(jnp.float32) + zrecv[v, 3].astype(jnp.float32)
+        out[pl.ds(v * rows, rows), :] = total.astype(jnp.bfloat16)
+
+    partner_sums(0)
+    arrived(coef.at[1], cf_recv.at[4])
+    send(coef.at[1], coef.at[3], cf_send.at[6], cf_recv.at[6], y_peer)
+    own_hidden(0)
+    pass_diagonal(1)
+    arrived(coef.at[2], cf_recv.at[5])
+    arrived(coef.at[3], cf_recv.at[6])
+    lane = lax.broadcasted_iota(jnp.int32, (4, 8, 128), 2)
+    for column in range(4):
+        block = coef[column]
+        for g in range(tokens.shape[0] // 8):
+            mine = jnp.sum(jnp.where(lane == 16 * g + w, block, 0.0), 2, keepdims=True)
+            mine = jnp.broadcast_to(mine, (4, 8, 128))
+            for at in range(4):
+                scale[g * 8 // rows, place(column, at), g % (rows // 8)] = mine[at]
+    loads[2].wait()
+    outputs(0, n)
+    send_half(0, n)
+    other_hidden(0)
+    outputs(0, 1 - n)
+    send_half(0, 1 - n)
+
+    gather_rest(1)
+    partner_sums(1)
+    relay_sums(0)
+    own_hidden(1)
+    column_sums(0)
+    outputs(1, n)
+    send_half(1, n)
+    other_hidden(1)
+    outputs(1, 1 - n)
+    send_half(1, 1 - n)
+    relay_sums(1)
+    column_sums(1)
+    finish(0)
+    finish(1)
+
+    for c in sent:
+        c.wait_send()
+    for v in range(WAVES):
+
+        @pl.loop(0, tiles)
+        def _(i):
+            lanes = pl.ds(pl.multiple_of(i * 128, 128), 128)
+            there = hid.at[v, n, :, lanes]
+            copy(gsend.at[v, i], grecv.at[v, i], g_send.at[v, i], g_recv.at[v, i], w, 1 - n).wait_send()
+            copy(there, there, h_send.at[v, i], h_recv.at[v, i], w, 1 - n).wait_send()
+
+
+def gather_plan(tokens, routes, route_weight, w_gate, w_up, w_down):
+    count = tokens.shape[0]
+    hidden, cols = w_gate.shape[1:]
+    tiles = hidden // 128
+    rows = count // WAVES
+    half = 8 * rows
+    bf16, f32 = jnp.bfloat16, jnp.float32
+    dma = pltpu.SemaphoreType.DMA
+    vmem = pl.BlockSpec(memory_space=pltpu.VMEM)
+    anywhere = pl.BlockSpec(memory_space=pl.ANY)
+    flops = 2 * 16 * count * hidden * cols * 3
+    return pl.pallas_call(
+        kernel,
+        out_shape=jax.ShapeDtypeStruct((count, cols), bf16),
+        in_specs=[anywhere, vmem, vmem, anywhere, anywhere, anywhere],
+        out_specs=vmem,
+        scratch_shapes=[
+            pltpu.VMEM((WAVES, 16, rows, cols), bf16),
+            pltpu.VMEM((tiles, 2, 128, cols), bf16),
+            pltpu.VMEM((hidden, cols), bf16),
+            pltpu.VMEM((4, 4, 8, 128), f32),
+            pltpu.VMEM((WAVES, 16, rows // 8, 8, 128), f32),
+            pltpu.VMEM((WAVES, tiles, half, 256), bf16),
+            pltpu.VMEM((WAVES, tiles, half, 256), bf16),
+            pltpu.VMEM((WAVES, 2, half, hidden), bf16),
+            pltpu.VMEM((WAVES, 16, rows, cols), bf16),
+            pltpu.VMEM((WAVES, 3, 4, rows, cols), bf16),
+            pltpu.VMEM((WAVES, 4, rows, cols), bf16),
+            pltpu.VMEM((WAVES, 4, rows, cols), bf16),
+            dma((3,)), dma((WAVES,)),
+            dma((WAVES, 4, 4)), dma((WAVES, 4, 4)),
+            dma((7,)), dma((7,)),
+            dma((WAVES, tiles)), dma((WAVES, tiles)),
+            dma((WAVES, tiles)), dma((WAVES, tiles)),
+            dma((WAVES, 3, 4)), dma((WAVES, 3, 4)),
+            dma((WAVES, 4)), dma((WAVES, 4)),
+        ],
+        compiler_params=pltpu.CompilerParams(
+            collective_id=0, has_side_effects=True, vmem_limit_bytes=52 * 1024 * 1024
+        ),
+        cost_estimate=pl.CostEstimate(
+            flops=flops, bytes_accessed=3 * hidden * cols * 2, transcendentals=8 * count * hidden
+        ),
+    )(
+        tokens, routes, route_weight,
+        w_gate.reshape(tiles, 128, cols), w_up.reshape(tiles, 128, cols), w_down[0],
+    )
+
+
 def solution(mesh):
+    chips = mesh.shape["wide"] == 16 and mesh.shape["narrow"] == 2
     return jax.shard_map(
-        on_device,
+        gather_plan if chips else slots_plan,
         mesh=mesh,
         in_specs=(
             P("wide", None),

time: 210 us -> 69.1 us (0.33); the launches traced: 207 us -> 68.9 us
  Pallas kernels: 0 us -> 65.7 us
  waiting for transfers between devices: 54.1 us -> 0 us
  local copies, waits for them, and re-layouts: 50.7 us -> 3.16 us
  blocking collectives: 46 us -> 0 us
  other arithmetic: 22.2 us -> 0 us
  matrix products: 13.8 us -> 0 us
  between operations: 13.5 us -> 0.01 us
  starting transfers between devices: 7 us -> 0 us
    pallas_call x0 -> x1, Pallas kernels: none -> 65.7 us  [gather_plan(): pl.pallas_call(kernel, out_shape=jax.ShapeDtypeStruct((count, cols), bf16...]
    all_to_all x1 -> x0, blocking collectives: 46 us -> none  [on_device(): lax.all_to_all(outgoing, 'wide', split_axis=0, concat_axis=1, tiled=True)]
    all_to_all x1 -> x0, waiting for transfers between devices: 31.6 us -> none  [on_device(): lax.all_to_all(expert_out, 'wide', split_axis=1, concat_axis=0, tiled=True)]
    unnamed x16 -> x5, local copies, waits for them, and re-layouts: 29.8 us -> 3.16 us
    dot_general x4 -> x0, matrix products: 13.8 us -> none  [the longest x1 4.9 us: on_device(): jnp.einsum('fs,fc->sc', lax.all_gather(hidden, 'narrow', axis=0, tiled=Tr...]
    all_gather x1 -> x0, waiting for transfers between devices: 12.1 us -> none  [on_device(): lax.all_gather(hidden, 'narrow', axis=0, tiled=True)]
    unnamed x1 -> x0, other arithmetic: 11.8 us -> none
    unnamed x3 -> x0, waiting for transfers between devices: 10.3 us -> none
  transfers between devices with their start and end apart: 3 -> 0, of which waited for: 3 -> 0; matrix products, arithmetic and copies ran while one was open for 0% -> 0% of each run, Pallas kernels for 0% -> 0%
where the time goes in v1:
time: 69.1 us; the launch traced here: 68.9 us
  Pallas kernels  65.7 us (95%)
  local copies, waits for them, and re-layouts  3.16 us (5%)
    pallas_call x1, Pallas kernels, gather_plan(): pl.pallas_call(kernel, out_shape=jax.ShapeDtypeStruct((count, cols), bf16...  65.7 us
    unnamed x5, local copies, waits for them, and re-layouts  3.16 us

profile of v1, /device:TPU:0, one launch (start us, length us, event | category | flops | bytes accessed | tf_op | source)
XLA Modules:
  0.0 68.9 jit_solution(8227669056474099739)
XLA Ops:
  0.0 0.8 %copy.7.routes = s32[64,6]{1,0:T(8,128)S(1)} copy(s32[64,6]{0,1:T(8,128)} %param.7) | data formatting | bytes 3072 | tf_op args[1]
  0.8 0.8 %copy.8.weights = f32[64,6]{1,0:T(8,128)S(1)} copy(f32[64,6]{0,1:T(8,128)} %param.8) | data formatting | bytes 3072 | tf_op args[2]
  1.6 0.0 copy-start
  1.6 0.9 %copy-done = bf16[64,2048]{1,0:T(8,128)(2,1)S(1)} copy-done((bf16[64,2048]{1,0:T(8,128)(2,1)S(1)}, bf16[64,2048]{1,0:T(8,128)(2,1)}, u32[]{:S(2)}) %copy-start) | copy-done | bytes 262168
  2.5 65.7 %shard_map.64 = bf16[64,1024]{1,0:T(8,128)(2,1)S(1)} custom-call(bf16[64,2048]{1,0:T(8,128)(2,1)S(1)} %copy-done, s32[64,6]{1,0:T(8,128)S(1)} %copy.7.routes, f32[64,6]{1,0:T(8,128)S(1)} %copy.8.weights, bf16[11,128,1024]{2,1,0:T(8,128)(2,1)} %bitcast.3, bf16[11,128,1024]{2,1,0:T(8,128)(2,1)} %bitcast.4, bf16[1408,1024]{1,0:T(8,128)(2,1)} %bitcast.5), custom_call_target="tpu_custom_call" | custom-call | flops 8858370048 | bytes 8650752 | tf_op jit(solution)/shard_map/pallas_call | solution.py:337
  68.2 0.7 copy.10
Async XLA Ops:
  1.6 0.9 %copy-start = (bf16[64,2048]{1,0:T(8,128)(2,1)S(1)}, bf16[64,2048]{1,0:T(8,128)(2,1)}, u32[]{:S(2)}) copy-start(bf16[64,2048]{1,0:T(8,128)(2,1)} %tokens.1) | copy-start | bytes 786436

commit v2 on v1

--- a/solution.py
+++ b/solution.py
@@ -1,5 +1,3 @@
-import functools
-
 import jax
 import jax.numpy as jnp
 from jax import lax
@@ -69,6 +67,7 @@
 
 
 WAVES = 2
+LAG = 3
 NT = (((1,), (1,)), ((), ()))
 NN = (((1,), (0,)), ((), ()))
 
@@ -166,12 +165,21 @@
     for c in own_copy + loads:
         c.start()
 
-    lane = lax.broadcasted_iota(jnp.int32, (8, 128), 1)
+    count = routes.shape[1]
+    diagonal = lax.broadcasted_iota(jnp.int32, (count, count), 0) == lax.broadcasted_iota(
+        jnp.int32, (count, count), 1
+    )
+
+    def as_column(row):
+        return jnp.sum(jnp.where(diagonal, jnp.broadcast_to(row, (count, count)), 0.0), 1, keepdims=True)
+
+    lane = lax.broadcasted_iota(jnp.int32, (8, 128), 1).astype(jnp.float32)
     packed = jnp.zeros((8, 128), jnp.float32)
-    for g in range(tokens.shape[0] // 8):
-        for k in range(routes.shape[1]):
-            chosen = routes[pl.ds(8 * g, 8), k : k + 1] + 16 * g
-            packed += jnp.where(lane == chosen, weights[pl.ds(8 * g, 8), k : k + 1], 0.0)
+    for k in range(routes.shape[0]):
+        chosen = as_column(routes[k : k + 1, :].astype(jnp.float32))
+        amount = as_column(weights[k : k + 1, :])
+        for g in range(count // 8):
+            packed += jnp.where(lane == chosen[8 * g : 8 * g + 8] + 16.0 * g, amount[8 * g : 8 * g + 8], 0.0)
     coef[0, z] = packed
     for k in (1, 2, 3):
         send(coef.at[0, z], coef.at[0, z], cf_send.at[k], cf_recv.at[z], z_peer(k))
@@ -192,27 +200,34 @@
     def tile(i):
         return gate_up[i].reshape(2 * gate_up.shape[2], cols)
 
-    def half(v, h):
-        return tok[v, pl.ds(8 * h, 8)].reshape(half_rows, cols)
-
-    def partner_sums(v):
-        @pl.loop(0, tiles)
-        def _(i):
-            sums = lax.dot_general(half(v, 1 - n), tile(i), NT, preferred_element_type=jnp.float32)
-            gsend[v, i] = sums.astype(jnp.bfloat16)
-            copy(gsend.at[v, i], grecv.at[v, i], g_send.at[v, i], g_recv.at[v, i], w, 1 - n).start()
-
-    def own_hidden(v):
-        @pl.loop(0, tiles)
-        def _(i):
-            sums = lax.dot_general(half(v, n), tile(i), NT, preferred_element_type=jnp.float32)
-            arrived(grecv.at[v, i], g_recv.at[v, i])
-            sums += grecv[v, i].astype(jnp.float32)
-            gate, up = sums[:, :128], sums[:, 128:]
-            lanes = pl.ds(pl.multiple_of(i * 128, 128), 128)
-            hid[v, n, :, lanes] = (gate / (1.0 + jnp.exp(-gate)) * up).astype(jnp.bfloat16)
-            there = hid.at[v, n, :, lanes]
-            copy(there, there, h_send.at[v, i], h_recv.at[v, i], w, 1 - n).start()
+    def add_tile(v, i):
+        x = tok[v].reshape(2 * half_rows, cols)
+        sums = lax.dot_general(x, tile(i), NT, preferred_element_type=jnp.float32)
+        gsend[v, i] = sums.astype(jnp.bfloat16).reshape(2, half_rows, 256)
+        copy(gsend.at[v, i, 1 - n], grecv.at[v, i], g_send.at[v, i], g_recv.at[v, i], w, 1 - n).start()
+
+    def hide_tile(v, i):
+        arrived(grecv.at[v, i], g_recv.at[v, i])
+        sums = gsend[v, i, n].astype(jnp.float32) + grecv[v, i].astype(jnp.float32)
+        gate, up = sums[:, :128], sums[:, 128:]
+        lanes = pl.ds(pl.multiple_of(i * 128, 128), 128)
+        hid[v, n, :, lanes] = (gate / (1.0 + jnp.exp(-gate)) * up).astype(jnp.bfloat16)
+        there = hid.at[v, n, :, lanes]
+        copy(there, there, h_send.at[v, i], h_recv.at[v, i], w, 1 - n).start()
+
+    def hidden_units(v):
+        @pl.loop(0, LAG)
+        def _(i):
+            add_tile(v, i)
+
+        @pl.loop(LAG, tiles)
+        def _(i):
+            add_tile(v, i)
+            hide_tile(v, i - LAG)
+
+        @pl.loop(tiles - LAG, tiles)
+        def _(i):
+            hide_tile(v, i)
 
     def outputs(v, h):
         column = scale[v, pl.ds(8 * h, 8)].reshape(half_rows, 128)[:, 0:1]
@@ -274,10 +289,9 @@
         total += zrecv[v, 2].astype(jnp.float32) + zrecv[v, 3].astype(jnp.float32)
         out[pl.ds(v * rows, rows), :] = total.astype(jnp.bfloat16)
 
-    partner_sums(0)
+    hidden_units(0)
     arrived(coef.at[1], cf_recv.at[4])
     send(coef.at[1], coef.at[3], cf_send.at[6], cf_recv.at[6], y_peer)
-    own_hidden(0)
     pass_diagonal(1)
     arrived(coef.at[2], cf_recv.at[5])
     arrived(coef.at[3], cf_recv.at[6])
@@ -297,9 +311,8 @@
     send_half(0, 1 - n)
 
     gather_rest(1)
-    partner_sums(1)
+    hidden_units(1)
     relay_sums(0)
-    own_hidden(1)
     column_sums(0)
     outputs(1, n)
     send_half(1, n)
@@ -319,7 +332,7 @@
         def _(i):
             lanes = pl.ds(pl.multiple_of(i * 128, 128), 128)
             there = hid.at[v, n, :, lanes]
-            copy(gsend.at[v, i], grecv.at[v, i], g_send.at[v, i], g_recv.at[v, i], w, 1 - n).wait_send()
+            copy(gsend.at[v, i, 1 - n], grecv.at[v, i], g_send.at[v, i], g_recv.at[v, i], w, 1 - n).wait_send()
             copy(there, there, h_send.at[v, i], h_recv.at[v, i], w, 1 - n).wait_send()
 
 
@@ -332,7 +345,7 @@
     bf16, f32 = jnp.bfloat16, jnp.float32
     dma = pltpu.SemaphoreType.DMA
     vmem = pl.BlockSpec(memory_space=pltpu.VMEM)
-    anywhere = pl.BlockSpec(memory_space=pl.ANY)
+    anywhere = pl.BlockSpec(memory_space=pltpu.HBM)
     flops = 2 * 16 * count * hidden * cols * 3
     return pl.pallas_call(
         kernel,
@@ -345,7 +358,7 @@
             pltpu.VMEM((hidden, cols), bf16),
             pltpu.VMEM((4, 4, 8, 128), f32),
             pltpu.VMEM((WAVES, 16, rows // 8, 8, 128), f32),
-            pltpu.VMEM((WAVES, tiles, half, 256), bf16),
+            pltpu.VMEM((WAVES, tiles, 2, half, 256), bf16),
             pltpu.VMEM((WAVES, tiles, half, 256), bf16),
             pltpu.VMEM((WAVES, 2, half, hidden), bf16),
             pltpu.VMEM((WAVES, 16, rows, cols), bf16),
@@ -367,7 +380,7 @@
             flops=flops, bytes_accessed=3 * hidden * cols * 2, transcendentals=8 * count * hidden
         ),
     )(
-        tokens, routes, route_weight,
+        tokens, routes.T, route_weight.T,
         w_gate.reshape(tiles, 128, cols), w_up.reshape(tiles, 128, cols), w_down[0],
     )
 

time: 69.1 us -> 72.5 us (1.049)
  Pallas kernels: 65.7 us -> 69.3 us
    pallas_call x1, Pallas kernels: 65.7 us -> 69.3 us  [gather_plan(): pl.pallas_call(kernel, out_shape=jax.ShapeDtypeStruct((count, cols), bf16...]
    unnamed x5 -> x7, local copies, waits for them, and re-layouts: 3.16 us -> 2.98 us
where the time goes in v2:
time: 72.5 us; the launch traced here: 72.3 us
  Pallas kernels  69.3 us (96%)
  local copies, waits for them, and re-layouts  2.98 us (4%)
    pallas_call x1, Pallas kernels, gather_plan(): pl.pallas_call(kernel, out_shape=jax.ShapeDtypeStruct((count, cols), bf16...  69.3 us
    unnamed x7, local copies, waits for them, and re-layouts  2.98 us

profile of v2, /device:TPU:0, one launch (start us, length us, event | category | flops | bytes accessed | tf_op | source)
XLA Modules:
  0.0 72.3 jit_solution(17615319919483629224)
XLA Ops:
  0.0 0.0 copy-start
  0.0 0.9 %copy-done = bf16[64,2048]{1,0:T(8,128)(2,1)S(1)} copy-done((bf16[64,2048]{1,0:T(8,128)(2,1)S(1)}, bf16[64,2048]{1,0:T(8,128)(2,1)}, u32[]{:S(2)}) %copy-start) | copy-done | bytes 262168
  1.0 0.0 copy-start.1
  1.0 0.7 copy-done.1
  1.6 0.0 copy-start.2
  1.6 0.7 copy-done.2
  2.3 69.3 %shard_map.64 = bf16[64,1024]{1,0:T(8,128)(2,1)S(1)} custom-call(bf16[64,2048]{1,0:T(8,128)(2,1)S(1)} %copy-done, s32[6,64]{1,0:T(8,128)S(1)} %bitcast.5, f32[6,64]{1,0:T(8,128)S(1)} %bitcast.6, bf16[11,128,1024]{2,1,0:T(8,128)(2,1)} %bitcast.7, bf16[11,128,1024]{2,1,0:T(8,128)(2,1)} %bitcast.8, bf16[1408,1024]{1,0:T(8,128)(2,1)} %bitcast.9), custom_call_target="tpu_custom_call" | custom-call | flops 8858370048 | bytes 8650752 | tf_op jit(solution)/shard_map/pallas_call | solution.py:350
  71.6 0.7 copy.8
Async XLA Ops:
  0.0 0.9 %copy-start = (bf16[64,2048]{1,0:T(8,128)(2,1)S(1)}, bf16[64,2048]{1,0:T(8,128)(2,1)}, u32[]{:S(2)}) copy-start(bf16[64,2048]{1,0:T(8,128)(2,1)} %tokens.1) | copy-start | bytes 786436
  1.0 0.7 copy-start.1
  1.6 0.7 copy-start.2

commit v3 on v2

--- a/solution.py
+++ b/solution.py
@@ -66,7 +66,7 @@
     return combined.astype(jnp.bfloat16)
 
 
-WAVES = 2
+WAVES = 4
 LAG = 3
 NT = (((1,), (1,)), ((), ()))
 NN = (((1,), (0,)), ((), ()))
@@ -77,8 +77,8 @@
 
 
 def kernel(
-    tokens, routes, weights, gate_hbm, up_hbm, down_hbm, out,
-    tok, gate_up, down, coef, scale, gsend, grecv, hid, part, back, zsend, zrecv,
+    tokens, routes_hbm, weights_hbm, gate_hbm, up_hbm, down_hbm, out,
+    routes, weights, tok, gate_up, down, coef, scale, gsend, grecv, hid, part, back, zsend, zrecv,
     load_sem, own_sem, ag_send, ag_recv, cf_send, cf_recv,
     g_send, g_recv, h_send, h_recv, rs_send, rs_recv, z_send, z_recv,
 ):
@@ -118,11 +118,15 @@
         pltpu.make_async_copy(gate_hbm, gate_up.at[:, 0], load_sem.at[0]),
         pltpu.make_async_copy(up_hbm, gate_up.at[:, 1], load_sem.at[1]),
         pltpu.make_async_copy(down_hbm, down, load_sem.at[2]),
+        pltpu.make_async_copy(routes_hbm, routes, load_sem.at[3]),
+        pltpu.make_async_copy(weights_hbm, weights, load_sem.at[4]),
     ]
     own_block = [tokens.at[pl.ds(v * rows, rows), pl.ds(pl.multiple_of(n * cols, cols), cols)] for v in range(WAVES)]
     own_copy = [
         pltpu.make_async_copy(own_block[v], tok.at[v, place(0, z)], own_sem.at[v]) for v in range(WAVES)
     ]
+    for c in loads[3:]:
+        c.start()
     pl.semaphore_wait(barrier, 6)
 
     def send_z(v):
@@ -141,15 +145,15 @@
             send_xy(v, block, from_z)
 
     def pass_diagonal(v):
-        for low in (0, 1):
-            for h in (0, 1):
-                from_z = 2 * h + low
-                block = tok.at[v, place(1 + h, from_z)]
-                arrived(block, ag_recv.at[v, 1 + h, from_z])
-                send(
-                    block, tok.at[v, place(3, from_z)], ag_send.at[v, 3, from_z], ag_recv.at[v, 3, from_z],
-                    y_peer if h == 0 else x_peer,
-                )
+        for k in (0, 1, 3, 2):
+            from_z = (z + k) % 4
+            h = from_z // 2
+            block = tok.at[v, place(1 + h, from_z)]
+            arrived(block, ag_recv.at[v, 1 + h, from_z])
+            send(
+                block, tok.at[v, place(3, from_z)], ag_send.at[v, 3, from_z], ag_recv.at[v, 3, from_z],
+                y_peer + h * (x_peer - y_peer),
+            )
 
     def gather_rest(v):
         for low in (0, 1):
@@ -159,11 +163,15 @@
                 arrived(tok.at[v, place(3, from_z)], ag_recv.at[v, 3, from_z])
         own_copy[v].wait()
 
-    send_z(0)
-    send_xy(0, own_block[0], z)
-    send_z(1)
-    for c in own_copy + loads:
+    def send_own(v):
+        send_z(v)
+        send_xy(v, own_block[v], z)
+
+    send_own(0)
+    for c in own_copy + loads[:3]:
         c.start()
+    for c in loads[3:]:
+        c.wait()
 
     count = routes.shape[1]
     diagonal = lax.broadcasted_iota(jnp.int32, (count, count), 0) == lax.broadcasted_iota(
@@ -185,9 +193,10 @@
         send(coef.at[0, z], coef.at[0, z], cf_send.at[k], cf_recv.at[z], z_peer(k))
 
     pass_column(0)
-    send_xy(1, own_block[1], z)
+    send_own(1)
     pass_diagonal(0)
     pass_column(1)
+    send_own(2)
     for k in (1, 2, 3):
         from_z = (z + k) % 4
         arrived(coef.at[0, from_z], cf_recv.at[from_z])
@@ -195,7 +204,6 @@
     send(coef.at[0], coef.at[2], cf_send.at[5], cf_recv.at[5], y_peer)
     for c in loads[:2]:
         c.wait()
-    gather_rest(0)
 
     def tile(i):
         return gate_up[i].reshape(2 * gate_up.shape[2], cols)
@@ -289,40 +297,61 @@
         total += zrecv[v, 2].astype(jnp.float32) + zrecv[v, 3].astype(jnp.float32)
         out[pl.ds(v * rows, rows), :] = total.astype(jnp.bfloat16)
 
+    def make_scale():
+        arrived(coef.at[2], cf_recv.at[5])
+        arrived(coef.at[3], cf_recv.at[6])
+        lane = lax.broadcasted_iota(jnp.int32, (4, 8, 128), 2)
+        for column in range(4):
+            block = coef[column]
+            for g in range(tokens.shape[0] // 8):
+                mine = jnp.sum(jnp.where(lane == 16 * g + w, block, 0.0), 2, keepdims=True)
+                mine = jnp.broadcast_to(mine, (4, 8, 128))
+                for at in range(4):
+                    scale[g * 8 // rows, place(column, at), g % (rows // 8)] = mine[at]
+
+    def give(v):
+        outputs(v, n)
+        send_half(v, n)
+        other_hidden(v)
+        outputs(v, 1 - n)
+        send_half(v, 1 - n)
+
+    gather_rest(0)
     hidden_units(0)
     arrived(coef.at[1], cf_recv.at[4])
     send(coef.at[1], coef.at[3], cf_send.at[6], cf_recv.at[6], y_peer)
     pass_diagonal(1)
-    arrived(coef.at[2], cf_recv.at[5])
-    arrived(coef.at[3], cf_recv.at[6])
-    lane = lax.broadcasted_iota(jnp.int32, (4, 8, 128), 2)
-    for column in range(4):
-        block = coef[column]
-        for g in range(tokens.shape[0] // 8):
-            mine = jnp.sum(jnp.where(lane == 16 * g + w, block, 0.0), 2, keepdims=True)
-            mine = jnp.broadcast_to(mine, (4, 8, 128))
-            for at in range(4):
-                scale[g * 8 // rows, place(column, at), g % (rows // 8)] = mine[at]
+    pass_column(2)
+    send_own(3)
+    make_scale()
     loads[2].wait()
-    outputs(0, n)
-    send_half(0, n)
-    other_hidden(0)
-    outputs(0, 1 - n)
-    send_half(0, 1 - n)
+    give(0)
 
     gather_rest(1)
     hidden_units(1)
+    pass_diagonal(2)
+    pass_column(3)
     relay_sums(0)
+    give(1)
+
+    gather_rest(2)
+    hidden_units(2)
+    pass_diagonal(3)
+    relay_sums(1)
     column_sums(0)
-    outputs(1, n)
-    send_half(1, n)
-    other_hidden(1)
-    outputs(1, 1 - n)
-    send_half(1, 1 - n)
-    relay_sums(1)
+    give(2)
+
+    gather_rest(3)
+    hidden_units(3)
+    relay_sums(2)
     column_sums(1)
-    finish(0)
-    finish(1)
+    give(3)
+
+    column_sums(2)
+    relay_sums(3)
+    column_sums(3)
+    for v in range(WAVES):
+        finish(v)
 
     for c in sent:
         c.wait_send()
@@ -345,14 +374,16 @@
     bf16, f32 = jnp.bfloat16, jnp.float32
     dma = pltpu.SemaphoreType.DMA
     vmem = pl.BlockSpec(memory_space=pltpu.VMEM)
-    anywhere = pl.BlockSpec(memory_space=pltpu.HBM)
+    anywhere = pl.BlockSpec(memory_space=pl.ANY)
     flops = 2 * 16 * count * hidden * cols * 3
     return pl.pallas_call(
         kernel,
         out_shape=jax.ShapeDtypeStruct((count, cols), bf16),
-        in_specs=[anywhere, vmem, vmem, anywhere, anywhere, anywhere],
+        in_specs=[anywhere] * 6,
         out_specs=vmem,
         scratch_shapes=[
+            pltpu.VMEM((route_weight.shape[1], count), jnp.int32),
+            pltpu.VMEM((route_weight.shape[1], count), f32),
             pltpu.VMEM((WAVES, 16, rows, cols), bf16),
             pltpu.VMEM((tiles, 2, 128, cols), bf16),
             pltpu.VMEM((hidden, cols), bf16),
@@ -365,7 +396,7 @@
             pltpu.VMEM((WAVES, 3, 4, rows, cols), bf16),
             pltpu.VMEM((WAVES, 4, rows, cols), bf16),
             pltpu.VMEM((WAVES, 4, rows, cols), bf16),
-            dma((3,)), dma((WAVES,)),
+            dma((5,)), dma((WAVES,)),
             dma((WAVES, 4, 4)), dma((WAVES, 4, 4)),
             dma((7,)), dma((7,)),
             dma((WAVES, tiles)), dma((WAVES, tiles)),
@@ -374,7 +405,7 @@
             dma((WAVES, 4)), dma((WAVES, 4)),
         ],
         compiler_params=pltpu.CompilerParams(
-            collective_id=0, has_side_effects=True, vmem_limit_bytes=52 * 1024 * 1024
+            collective_id=0, has_side_effects=True, vmem_limit_bytes=64 * 1024 * 1024 - 128 * 1024
         ),
         cost_estimate=pl.CostEstimate(
             flops=flops, bytes_accessed=3 * hidden * cols * 2, transcendentals=8 * count * hidden

time: 72.5 us -> 71.1 us (0.981)
  local copies, waits for them, and re-layouts: 2.98 us -> 1.57 us
    unnamed x7 -> x1, local copies, waits for them, and re-layouts: 2.98 us -> 1.57 us
where the time goes in v3:
time: 71.1 us; the launch traced here: 71 us
  Pallas kernels  69.4 us (98%)
  local copies, waits for them, and re-layouts  1.57 us (2%)
    pallas_call x1, Pallas kernels, gather_plan(): pl.pallas_call(kernel, out_shape=jax.ShapeDtypeStruct((count, cols), bf16...  69.4 us
    unnamed x1, local copies, waits for them, and re-layouts  1.57 us

profile of v3, /device:TPU:0, one launch (start us, length us, event | category | flops | bytes accessed | tf_op | source)
XLA Modules:
  0.0 71.0 jit_solution(13523898021974637862)
XLA Ops:
  0.0 69.4 %shard_map.64 = bf16[64,1024]{1,0:T(8,128)(2,1)} custom-call(bf16[64,2048]{1,0:T(8,128)(2,1)} %tokens.1, s32[6,64]{1,0:T(8,128)} %bitcast.8, f32[6,64]{1,0:T(8,128)} %bitcast.9, bf16[11,128,1024]{2,1,0:T(8,128)(2,1)} %bitcast.5, bf16[11,128,1024]{2,1,0:T(8,128)(2,1)} %bitcast.6, bf16[1408,1024]{1,0:T(8,128)(2,1)} %bitcast.7), custom_call_target="tpu_custom_call" | custom-call | flops 8858370048 | bytes 8650752 | tf_op jit(solution)/shard_map/pallas_call | solution.py:379
  69.4 1.6 %copy.8 = bf16[64,1024]{1,0:T(8,128)(2,1)} copy(bf16[64,1024]{1,0:T(8,128)(2,1)} %shard_map.64) | data formatting | bytes 262144

commit v4 on v3

--- a/solution.py
+++ b/solution.py
@@ -68,7 +68,6 @@
 
 WAVES = 4
 LAG = 3
-NT = (((1,), (1,)), ((), ()))
 NN = (((1,), (0,)), ((), ()))
 
 
@@ -78,7 +77,7 @@
 
 def kernel(
     tokens, routes_hbm, weights_hbm, gate_hbm, up_hbm, down_hbm, out,
-    routes, weights, tok, gate_up, down, coef, scale, gsend, grecv, hid, part, back, zsend, zrecv,
+    routes, weights, tok, gate_up, gate_up_t, down, coef, scale, gsend, grecv, hid, part, back, zsend, zrecv,
     load_sem, own_sem, ag_send, ag_recv, cf_send, cf_recv,
     g_send, g_recv, h_send, h_recv, rs_send, rs_recv, z_send, z_recv,
 ):
@@ -163,15 +162,18 @@
                 arrived(tok.at[v, place(3, from_z)], ag_recv.at[v, 3, from_z])
         own_copy[v].wait()
 
-    def send_own(v):
-        send_z(v)
+    send_z(0)
+    for v in range(WAVES):
         send_xy(v, own_block[v], z)
-
-    send_own(0)
     for c in own_copy + loads[:3]:
         c.start()
     for c in loads[3:]:
         c.wait()
+
+    def turn_tiles(first, last):
+        @pl.loop(first, last)
+        def _(i):
+            gate_up_t[i] = gate_up[i].reshape(256, cols).T
 
     count = routes.shape[1]
     diagonal = lax.broadcasted_iota(jnp.int32, (count, count), 0) == lax.broadcasted_iota(
@@ -192,25 +194,26 @@
     for k in (1, 2, 3):
         send(coef.at[0, z], coef.at[0, z], cf_send.at[k], cf_recv.at[z], z_peer(k))
 
+    for c in loads[:2]:
+        c.wait()
+    turn_tiles(0, 3)
     pass_column(0)
-    send_own(1)
+    send_z(1)
+    turn_tiles(3, 6)
     pass_diagonal(0)
+    turn_tiles(6, 8)
     pass_column(1)
-    send_own(2)
+    send_z(2)
     for k in (1, 2, 3):
         from_z = (z + k) % 4
         arrived(coef.at[0, from_z], cf_recv.at[from_z])
     send(coef.at[0], coef.at[1], cf_send.at[4], cf_recv.at[4], x_peer)
     send(coef.at[0], coef.at[2], cf_send.at[5], cf_recv.at[5], y_peer)
-    for c in loads[:2]:
-        c.wait()
-
-    def tile(i):
-        return gate_up[i].reshape(2 * gate_up.shape[2], cols)
+    turn_tiles(8, tiles)
 
     def add_tile(v, i):
         x = tok[v].reshape(2 * half_rows, cols)
-        sums = lax.dot_general(x, tile(i), NT, preferred_element_type=jnp.float32)
+        sums = lax.dot_general(x, gate_up_t[i], NN, preferred_element_type=jnp.float32)
         gsend[v, i] = sums.astype(jnp.bfloat16).reshape(2, half_rows, 256)
         copy(gsend.at[v, i, 1 - n], grecv.at[v, i], g_send.at[v, i], g_recv.at[v, i], w, 1 - n).start()
 
@@ -223,7 +226,7 @@
         there = hid.at[v, n, :, lanes]
         copy(there, there, h_send.at[v, i], h_recv.at[v, i], w, 1 - n).start()
 
-    def hidden_units(v):
+    def hidden_units(v, meanwhile):
         @pl.loop(0, LAG)
         def _(i):
             add_tile(v, i)
@@ -232,6 +235,8 @@
         def _(i):
             add_tile(v, i)
             hide_tile(v, i - LAG)
+
+        meanwhile()
 
         @pl.loop(tiles - LAG, tiles)
         def _(i):
@@ -316,34 +321,39 @@
         outputs(v, 1 - n)
         send_half(v, 1 - n)
 
+    def between_0():
+        arrived(coef.at[1], cf_recv.at[4])
+        send(coef.at[1], coef.at[3], cf_send.at[6], cf_recv.at[6], y_peer)
+        pass_diagonal(1)
+        pass_column(2)
+        send_z(3)
+
+    def between_1():
+        pass_diagonal(2)
+        pass_column(3)
+        relay_sums(0)
+
+    def between_2():
+        pass_diagonal(3)
+        relay_sums(1)
+
     gather_rest(0)
-    hidden_units(0)
-    arrived(coef.at[1], cf_recv.at[4])
-    send(coef.at[1], coef.at[3], cf_send.at[6], cf_recv.at[6], y_peer)
-    pass_diagonal(1)
-    pass_column(2)
-    send_own(3)
+    hidden_units(0, between_0)
     make_scale()
     loads[2].wait()
     give(0)
 
     gather_rest(1)
-    hidden_units(1)
-    pass_diagonal(2)
-    pass_column(3)
-    relay_sums(0)
+    hidden_units(1, between_1)
     give(1)
 
     gather_rest(2)
-    hidden_units(2)
-    pass_diagonal(3)
-    relay_sums(1)
+    hidden_units(2, between_2)
     column_sums(0)
     give(2)
 
     gather_rest(3)
-    hidden_units(3)
-    relay_sums(2)
+    hidden_units(3, lambda: relay_sums(2))
     column_sums(1)
     give(3)
 
@@ -386,6 +396,7 @@
             pltpu.VMEM((route_weight.shape[1], count), f32),
             pltpu.VMEM((WAVES, 16, rows, cols), bf16),
             pltpu.VMEM((tiles, 2, 128, cols), bf16),
+            pltpu.VMEM((tiles, cols, 256), bf16),
             pltpu.VMEM((hidden, cols), bf16),
             pltpu.VMEM((4, 4, 8, 128), f32),
             pltpu.VMEM((WAVES, 16, rows // 8, 8, 128), f32),

time: 71.1 us -> 67.2 us (0.945)
  Pallas kernels: 69.4 us -> 65.5 us
    pallas_call x1, Pallas kernels: 69.4 us -> 65.5 us  [gather_plan(): pl.pallas_call(kernel, out_shape=jax.ShapeDtypeStruct((count, cols), bf16...]
where the time goes in v4:
time: 67.2 us; the launch traced here: 67.1 us
  Pallas kernels  65.5 us (97%)
  local copies, waits for them, and re-layouts  1.57 us (2%)
    pallas_call x1, Pallas kernels, gather_plan(): pl.pallas_call(kernel, out_shape=jax.ShapeDtypeStruct((count, cols), bf16...  65.5 us
    unnamed x1, local copies, waits for them, and re-layouts  1.57 us

profile of v4, /device:TPU:0, one launch (start us, length us, event | category | flops | bytes accessed | tf_op | source)
XLA Modules:
  0.0 67.1 jit_solution(17728575006894664498)
XLA Ops:
  0.0 65.5 %shard_map.64 = bf16[64,1024]{1,0:T(8,128)(2,1)} custom-call(bf16[64,2048]{1,0:T(8,128)(2,1)} %tokens.1, s32[6,64]{1,0:T(8,128)} %bitcast.8, f32[6,64]{1,0:T(8,128)} %bitcast.9, bf16[11,128,1024]{2,1,0:T(8,128)(2,1)} %bitcast.5, bf16[11,128,1024]{2,1,0:T(8,128)(2,1)} %bitcast.6, bf16[1408,1024]{1,0:T(8,128)(2,1)} %bitcast.7), custom_call_target="tpu_custom_call" | custom-call | flops 8858370048 | bytes 8650752 | tf_op jit(solution)/shard_map/pallas_call | solution.py:389
  65.5 1.6 %copy.8 = bf16[64,1024]{1,0:T(8,128)(2,1)} copy(bf16[64,1024]{1,0:T(8,128)(2,1)} %shard_map.64) | data formatting | bytes 262144

commit v5 on v4

--- a/solution.py
+++ b/solution.py
@@ -67,7 +67,6 @@
 
 
 WAVES = 4
-LAG = 3
 NN = (((1,), (0,)), ((), ()))
 
 
@@ -211,45 +210,48 @@
     send(coef.at[0], coef.at[2], cf_send.at[5], cf_recv.at[5], y_peer)
     turn_tiles(8, tiles)
 
-    def add_tile(v, i):
+    def step(v, later, earlier):
         x = tok[v].reshape(2 * half_rows, cols)
-        sums = lax.dot_general(x, gate_up_t[i], NN, preferred_element_type=jnp.float32)
-        gsend[v, i] = sums.astype(jnp.bfloat16).reshape(2, half_rows, 256)
-        copy(gsend.at[v, i, 1 - n], grecv.at[v, i], g_send.at[v, i], g_recv.at[v, i], w, 1 - n).start()
-
-    def hide_tile(v, i):
-        arrived(grecv.at[v, i], g_recv.at[v, i])
-        sums = gsend[v, i, n].astype(jnp.float32) + grecv[v, i].astype(jnp.float32)
-        gate, up = sums[:, :128], sums[:, 128:]
-        lanes = pl.ds(pl.multiple_of(i * 128, 128), 128)
-        hid[v, n, :, lanes] = (gate / (1.0 + jnp.exp(-gate)) * up).astype(jnp.bfloat16)
-        there = hid.at[v, n, :, lanes]
-        copy(there, there, h_send.at[v, i], h_recv.at[v, i], w, 1 - n).start()
+        for j in earlier:
+            arrived(grecv.at[v, j], g_recv.at[v, j])
+        sums = [lax.dot_general(x, gate_up_t[i], NN, preferred_element_type=jnp.float32) for i in later]
+        hidden = []
+        for j in earlier:
+            total = gsend[v, j, n].astype(jnp.float32) + grecv[v, j].astype(jnp.float32)
+            gate, up = total[:, :128], total[:, 128:]
+            hidden.append((gate / (1.0 + jnp.exp(-gate)) * up).astype(jnp.bfloat16))
+        for i, value in zip(later, sums):
+            gsend[v, i] = value.astype(jnp.bfloat16).reshape(2, half_rows, 256)
+        places = [hid.at[v, n, :, pl.ds(pl.multiple_of(j * 128, 128), 128)] for j in earlier]
+        for there, value in zip(places, hidden):
+            there[...] = value
+        for i in later:
+            copy(gsend.at[v, i, 1 - n], grecv.at[v, i], g_send.at[v, i], g_recv.at[v, i], w, 1 - n).start()
+        for j, there in zip(earlier, places):
+            copy(there, there, h_send.at[v, j], h_recv.at[v, j], w, 1 - n).start()
 
     def hidden_units(v, meanwhile):
-        @pl.loop(0, LAG)
+        lead = 2 + tiles % 2
+        step(v, range(lead), ())
+
+        @pl.loop(0, (tiles - lead) // 2)
         def _(i):
-            add_tile(v, i)
-
-        @pl.loop(LAG, tiles)
+            step(v, (2 * i + lead, 2 * i + lead + 1), (2 * i, 2 * i + 1))
+
+        meanwhile()
+        step(v, (), range(tiles - lead, tiles))
+
+    def outputs(v, first, halves):
+        column = scale[v, pl.ds(8 * first, 8 * halves)].reshape(halves * half_rows, 128)[:, 0:1]
+        units = hid[v, pl.ds(first, halves)].reshape(halves * half_rows, hid.shape[3])
+
+        @pl.loop(0, cols // 512)
         def _(i):
-            add_tile(v, i)
-            hide_tile(v, i - LAG)
-
-        meanwhile()
-
-        @pl.loop(tiles - LAG, tiles)
-        def _(i):
-            hide_tile(v, i)
-
-    def outputs(v, h):
-        column = scale[v, pl.ds(8 * h, 8)].reshape(half_rows, 128)[:, 0:1]
-
-        @pl.loop(0, cols // 256)
-        def _(i):
-            lanes = pl.ds(pl.multiple_of(i * 256, 256), 256)
-            acc = lax.dot_general(hid[v, h], down[:, lanes], NN, preferred_element_type=jnp.float32)
-            part[v, pl.ds(8 * h, 8), :, lanes] = (acc * column).astype(jnp.bfloat16).reshape(8, rows, 256)
+            lanes = pl.ds(pl.multiple_of(i * 512, 512), 512)
+            acc = lax.dot_general(units, down[:, lanes], NN, preferred_element_type=jnp.float32)
+            part[v, pl.ds(8 * first, 8 * halves), :, lanes] = (
+                (acc * column).astype(jnp.bfloat16).reshape(8 * halves, rows, 512)
+            )
 
     def other_hidden(v):
         @pl.loop(0, tiles)
@@ -315,10 +317,9 @@
                     scale[g * 8 // rows, place(column, at), g % (rows // 8)] = mine[at]
 
     def give(v):
-        outputs(v, n)
+        other_hidden(v)
+        outputs(v, 0, 2)
         send_half(v, n)
-        other_hidden(v)
-        outputs(v, 1 - n)
         send_half(v, 1 - n)
 
     def between_0():
@@ -355,7 +356,11 @@
     gather_rest(3)
     hidden_units(3, lambda: relay_sums(2))
     column_sums(1)
-    give(3)
+    outputs(3, n, 1)
+    send_half(3, n)
+    other_hidden(3)
+    outputs(3, 1 - n, 1)
+    send_half(3, 1 - n)
 
     column_sums(2)
     relay_sums(3)

time: 67.2 us -> 75.6 us (1.12)
  Pallas kernels: 65.5 us -> 73.9 us
    pallas_call x1, Pallas kernels: 65.5 us -> 73.9 us  [gather_plan(): pl.pallas_call(kernel, out_shape=jax.ShapeDtypeStruct((count, cols), bf16...]
where the time goes in v5:
time: 75.6 us; the launch traced here: 75.5 us
  Pallas kernels  73.9 us (98%)
  local copies, waits for them, and re-layouts  1.57 us (2%)
    pallas_call x1, Pallas kernels, gather_plan(): pl.pallas_call(kernel, out_shape=jax.ShapeDtypeStruct((count, cols), bf16...  73.9 us
    unnamed x1, local copies, waits for them, and re-layouts  1.57 us

profile of v5, /device:TPU:0, one launch (start us, length us, event | category | flops | bytes accessed | tf_op | source)
XLA Modules:
  0.0 75.5 jit_solution(5290386146369820099)
XLA Ops:
  0.0 73.9 %shard_map.64 = bf16[64,1024]{1,0:T(8,128)(2,1)} custom-call(bf16[64,2048]{1,0:T(8,128)(2,1)} %tokens.1, s32[6,64]{1,0:T(8,128)} %bitcast.8, f32[6,64]{1,0:T(8,128)} %bitcast.9, bf16[11,128,1024]{2,1,0:T(8,128)(2,1)} %bitcast.5, bf16[11,128,1024]{2,1,0:T(8,128)(2,1)} %bitcast.6, bf16[1408,1024]{1,0:T(8,128)(2,1)} %bitcast.7), custom_call_target="tpu_custom_call" | custom-call | flops 8858370048 | bytes 8650752 | tf_op jit(solution)/shard_map/pallas_call | solution.py:394
  73.9 1.6 %copy.8 = bf16[64,1024]{1,0:T(8,128)(2,1)} copy(bf16[64,1024]{1,0:T(8,128)(2,1)} %shard_map.64) | data formatting | bytes 262144

commit v6 on v4

--- a/solution.py
+++ b/solution.py
@@ -67,7 +67,6 @@
 
 
 WAVES = 4
-LAG = 3
 NN = (((1,), (0,)), ((), ()))
 
 
@@ -211,36 +210,31 @@
     send(coef.at[0], coef.at[2], cf_send.at[5], cf_recv.at[5], y_peer)
     turn_tiles(8, tiles)
 
-    def add_tile(v, i):
-        x = tok[v].reshape(2 * half_rows, cols)
-        sums = lax.dot_general(x, gate_up_t[i], NN, preferred_element_type=jnp.float32)
-        gsend[v, i] = sums.astype(jnp.bfloat16).reshape(2, half_rows, 256)
-        copy(gsend.at[v, i, 1 - n], grecv.at[v, i], g_send.at[v, i], g_recv.at[v, i], w, 1 - n).start()
-
-    def hide_tile(v, i):
-        arrived(grecv.at[v, i], g_recv.at[v, i])
-        sums = gsend[v, i, n].astype(jnp.float32) + grecv[v, i].astype(jnp.float32)
-        gate, up = sums[:, :128], sums[:, 128:]
-        lanes = pl.ds(pl.multiple_of(i * 128, 128), 128)
-        hid[v, n, :, lanes] = (gate / (1.0 + jnp.exp(-gate)) * up).astype(jnp.bfloat16)
-        there = hid.at[v, n, :, lanes]
-        copy(there, there, h_send.at[v, i], h_recv.at[v, i], w, 1 - n).start()
+    def half(v, h):
+        return tok[v, pl.ds(8 * h, 8)].reshape(half_rows, cols)
+
+    def partner_sums(v):
+        @pl.loop(0, tiles)
+        def _(i):
+            sums = lax.dot_general(half(v, 1 - n), gate_up_t[i], NN, preferred_element_type=jnp.float32)
+            gsend[v, i] = sums.astype(jnp.bfloat16)
+            copy(gsend.at[v, i], grecv.at[v, i], g_send.at[v, i], g_recv.at[v, i], w, 1 - n).start()
+
+    def own_hidden(v):
+        @pl.loop(0, tiles)
+        def _(i):
+            sums = lax.dot_general(half(v, n), gate_up_t[i], NN, preferred_element_type=jnp.float32)
+            arrived(grecv.at[v, i], g_recv.at[v, i])
+            sums += grecv[v, i].astype(jnp.float32)
+            gate, up = sums[:, :128], sums[:, 128:]
+            there = hid.at[v, n, :, pl.ds(pl.multiple_of(i * 128, 128), 128)]
+            there[...] = (gate / (1.0 + jnp.exp(-gate)) * up).astype(jnp.bfloat16)
+            copy(there, there, h_send.at[v, i], h_recv.at[v, i], w, 1 - n).start()
 
     def hidden_units(v, meanwhile):
-        @pl.loop(0, LAG)
-        def _(i):
-            add_tile(v, i)
-
-        @pl.loop(LAG, tiles)
-        def _(i):
-            add_tile(v, i)
-            hide_tile(v, i - LAG)
-
+        partner_sums(v)
         meanwhile()
-
-        @pl.loop(tiles - LAG, tiles)
-        def _(i):
-            hide_tile(v, i)
+        own_hidden(v)
 
     def outputs(v, h):
         column = scale[v, pl.ds(8 * h, 8)].reshape(half_rows, 128)[:, 0:1]
@@ -371,7 +365,7 @@
         def _(i):
             lanes = pl.ds(pl.multiple_of(i * 128, 128), 128)
             there = hid.at[v, n, :, lanes]
-            copy(gsend.at[v, i, 1 - n], grecv.at[v, i], g_send.at[v, i], g_recv.at[v, i], w, 1 - n).wait_send()
+            copy(gsend.at[v, i], grecv.at[v, i], g_send.at[v, i], g_recv.at[v, i], w, 1 - n).wait_send()
             copy(there, there, h_send.at[v, i], h_recv.at[v, i], w, 1 - n).wait_send()
 
 
@@ -400,7 +394,7 @@
             pltpu.VMEM((hidden, cols), bf16),
             pltpu.VMEM((4, 4, 8, 128), f32),
             pltpu.VMEM((WAVES, 16, rows // 8, 8, 128), f32),
-            pltpu.VMEM((WAVES, tiles, 2, half, 256), bf16),
+            pltpu.VMEM((WAVES, tiles, half, 256), bf16),
             pltpu.VMEM((WAVES, tiles, half, 256), bf16),
             pltpu.VMEM((WAVES, 2, half, hidden), bf16),
             pltpu.VMEM((WAVES, 16, rows, cols), bf16),

time: 67.2 us -> 71.7 us (1.067)
  Pallas kernels: 65.5 us -> 70 us
    pallas_call x1, Pallas kernels: 65.5 us -> 70 us  [gather_plan(): pl.pallas_call(kernel, out_shape=jax.ShapeDtypeStruct((count, cols), bf16...]
where the time goes in v6:
time: 71.7 us; the launch traced here: 71.6 us
  Pallas kernels  70 us (98%)
  local copies, waits for them, and re-layouts  1.57 us (2%)
    pallas_call x1, Pallas kernels, gather_plan(): pl.pallas_call(kernel, out_shape=jax.ShapeDtypeStruct((count, cols), bf16...  70 us
    unnamed x1, local copies, waits for them, and re-layouts  1.57 us

profile of v6, /device:TPU:0, one launch (start us, length us, event | category | flops | bytes accessed | tf_op | source)
XLA Modules:
  0.0 71.6 jit_solution(13820540401438143367)
XLA Ops:
  0.0 70.0 %shard_map.64 = bf16[64,1024]{1,0:T(8,128)(2,1)} custom-call(bf16[64,2048]{1,0:T(8,128)(2,1)} %tokens.1, s32[6,64]{1,0:T(8,128)} %bitcast.8, f32[6,64]{1,0:T(8,128)} %bitcast.9, bf16[11,128,1024]{2,1,0:T(8,128)(2,1)} %bitcast.5, bf16[11,128,1024]{2,1,0:T(8,128)(2,1)} %bitcast.6, bf16[1408,1024]{1,0:T(8,128)(2,1)} %bitcast.7), custom_call_target="tpu_custom_call" | custom-call | flops 8858370048 | bytes 8650752 | tf_op jit(solution)/shard_map/pallas_call | solution.py:383
  70.0 1.6 %copy.8 = bf16[64,1024]{1,0:T(8,128)(2,1)} copy(bf16[64,1024]{1,0:T(8,128)(2,1)} %shard_map.64) | data formatting | bytes 262144

commit v7 on v4

--- a/solution.py
+++ b/solution.py
@@ -226,17 +226,26 @@
         there = hid.at[v, n, :, lanes]
         copy(there, there, h_send.at[v, i], h_recv.at[v, i], w, 1 - n).start()
 
-    def hidden_units(v, meanwhile):
+    def hidden_units(v, first, second, third):
         @pl.loop(0, LAG)
         def _(i):
             add_tile(v, i)
 
-        @pl.loop(LAG, tiles)
+        first()
+
+        @pl.loop(LAG, LAG + (tiles - LAG) // 2)
         def _(i):
             add_tile(v, i)
             hide_tile(v, i - LAG)
 
-        meanwhile()
+        second()
+
+        @pl.loop(LAG + (tiles - LAG) // 2, tiles)
+        def _(i):
+            add_tile(v, i)
+            hide_tile(v, i - LAG)
+
+        third()
 
         @pl.loop(tiles - LAG, tiles)
         def _(i):
@@ -321,40 +330,34 @@
         outputs(v, 1 - n)
         send_half(v, 1 - n)
 
-    def between_0():
+    def coef_diagonal():
         arrived(coef.at[1], cf_recv.at[4])
         send(coef.at[1], coef.at[3], cf_send.at[6], cf_recv.at[6], y_peer)
+
+    def first_0():
         pass_diagonal(1)
         pass_column(2)
         send_z(3)
 
-    def between_1():
-        pass_diagonal(2)
-        pass_column(3)
-        relay_sums(0)
-
-    def between_2():
-        pass_diagonal(3)
-        relay_sums(1)
+    def nothing():
+        pass
 
     gather_rest(0)
-    hidden_units(0, between_0)
+    hidden_units(0, first_0, coef_diagonal, lambda: pass_column(3))
     make_scale()
     loads[2].wait()
     give(0)
 
     gather_rest(1)
-    hidden_units(1, between_1)
+    hidden_units(1, lambda: pass_diagonal(2), lambda: relay_sums(0), lambda: pass_diagonal(3))
     give(1)
 
     gather_rest(2)
-    hidden_units(2, between_2)
-    column_sums(0)
+    hidden_units(2, lambda: relay_sums(1), lambda: column_sums(0), nothing)
     give(2)
 
     gather_rest(3)
-    hidden_units(3, lambda: relay_sums(2))
-    column_sums(1)
+    hidden_units(3, nothing, lambda: relay_sums(2), lambda: column_sums(1))
     give(3)
 
     column_sums(2)

time: 67.2 us -> 71.8 us (1.068)
  Pallas kernels: 65.5 us -> 70 us
    pallas_call x1, Pallas kernels: 65.5 us -> 70 us  [gather_plan(): pl.pallas_call(kernel, out_shape=jax.ShapeDtypeStruct((count, cols), bf16...]
where the time goes in v7:
time: 71.8 us; the launch traced here: 71.6 us
  Pallas kernels  70 us (97%)
  local copies, waits for them, and re-layouts  1.57 us (2%)
    pallas_call x1, Pallas kernels, gather_plan(): pl.pallas_call(kernel, out_shape=jax.ShapeDtypeStruct((count, cols), bf16...  70 us
    unnamed x1, local copies, waits for them, and re-layouts  1.57 us

profile of v7, /device:TPU:0, one launch (start us, length us, event | category | flops | bytes accessed | tf_op | source)
XLA Modules:
  0.0 71.6 jit_solution(3046480188245971450)
XLA Ops:
  0.0 70.0 %shard_map.64 = bf16[64,1024]{1,0:T(8,128)(2,1)} custom-call(bf16[64,2048]{1,0:T(8,128)(2,1)} %tokens.1, s32[6,64]{1,0:T(8,128)} %bitcast.8, f32[6,64]{1,0:T(8,128)} %bitcast.9, bf16[11,128,1024]{2,1,0:T(8,128)(2,1)} %bitcast.5, bf16[11,128,1024]{2,1,0:T(8,128)(2,1)} %bitcast.6, bf16[1408,1024]{1,0:T(8,128)(2,1)} %bitcast.7), custom_call_target="tpu_custom_call" | custom-call | flops 8858370048 | bytes 8650752 | tf_op jit(solution)/shard_map/pallas_call | solution.py:392
  70.1 1.6 %copy.8 = bf16[64,1024]{1,0:T(8,128)(2,1)} copy(bf16[64,1024]{1,0:T(8,128)(2,1)} %shard_map.64) | data formatting | bytes 262144
